TPU v7x, 32 devices: a whole 2x2x4 slice. The times are simulated.
32 devices in a mesh: groups: 2 (over y), row: 4 (over x, core), col: 4 (over z).
Axes of the slice: x: 2, y: 2, z: 4, core: 2. Of those that a mesh axis runs over, the one named last changes fastest.
Arguments:
- features: float32 [16384, 256], P(('groups', 'row', 'col')), parts along dimension 0, may hold values from -6 to 6
- weight: float32 [256, 256], replicated, may hold values from -0.375 to 0.375
- cotangent: float32 [16384, 256], P(('groups', 'row', 'col')), parts along dimension 0, may hold values from -6 to 6
- column_of: int32 [16384, 1], P(('groups', 'row', 'col')), parts along dimension 0, may hold values from 0 to 3; in each aligned block of 512 rows (0 to 511, 512 to 1023, ...) at most 256 rows name the same one
- block_rows: int32 [32, 32], P(('groups', 'row', 'col')), parts along dimension 0, may hold values from 0 to 15
- block_cols: int32 [32, 32], P(('groups', 'row', 'col')), parts along dimension 0, may hold values from 0 to 7
- edge_blocks: float32 [32, 32, 128, 128], P(('groups', 'row', 'col')), parts along dimension 0, may hold values from -0.25 to 0.25
Outputs:
- activated: float32 [16384, 256], P(('groups', 'row', 'col')), parts along dimension 0
- input_grad: float32 [16384, 256], P(('groups', 'row', 'col')), parts along dimension 0
- weight_grad: float32 [512, 256], P('groups'), parts along dimension 0
There are 2 independent parts, one for each index of `groups`. A program takes and returns all parts, laid end to end along the dimension named above; an argument that names none is the same for every part. Nothing has to cross between parts.
Inputs may be any that keep to these rules, and one draw needn't show every extreme that they name: `column_of`: among the 512 rows of one device no grid column is named by more than 256 rows, and on some devices some grid column by exactly 256. `block_rows`: A pair of destination and source block may be listed more than once in a tile; the listed blocks then add.
All inputs are finite; a program needn't handle non-finite values.
Results may differ from a plain program's by a relative error of at most 0.0003.
Values sent between devices are 32-bit elements; how exact they have to be, the bound alone decides.
A program may use at most 64 MiB of HBM per device.

v0:
```python
import jax
import jax.numpy as jnp
from jax import lax
from jax.sharding import PartitionSpec as P

precise = lax.Precision.HIGHEST


def activate(value):
    return jax.nn.gelu(value, approximate=True)


def local(features, weight, cotangent, column_of, block_rows, block_cols, edge_blocks):
    row_count, feat_width = features.shape
    block_size = edge_blocks.shape[2]
    col_count = lax.axis_size("col")
    grid_rows = lax.axis_size("row")
    capacity = max(2, 2 * row_count // col_count)
    dest_blocks = grid_rows * row_count // block_size
    source_blocks = col_count * capacity // block_size
    target = column_of[:, 0]
    onehot = (target[:, None] == jnp.arange(col_count, dtype=jnp.int32)[None, :]).astype(jnp.int32)
    slot_rank = jnp.sum((jnp.cumsum(onehot, axis=0) - onehot) * onehot, axis=1)
    slot_index = target * capacity + slot_rank
    tile_rows = block_rows[0]
    tile_cols = block_cols[0]
    tile_edges = edge_blocks[0]
    dest_select = (tile_rows[None, :] == jnp.arange(dest_blocks, dtype=jnp.int32)[:, None]).astype(
        jnp.float32
    )
    source_select = (
        tile_cols[None, :] == jnp.arange(source_blocks, dtype=jnp.int32)[:, None]
    ).astype(jnp.float32)
    outgoing = jnp.dot(features, weight, precision=precise, preferred_element_type=jnp.float32)
    buffer = jnp.zeros((col_count * capacity, feat_width), jnp.float32).at[slot_index].set(outgoing)
    arrived = lax.all_to_all(
        buffer.reshape(col_count, capacity, feat_width),
        "col",
        split_axis=0,
        concat_axis=0,
        tiled=True,
    )
    slot_blocks = arrived.reshape(source_blocks, block_size, feat_width)
    picked = slot_blocks[tile_cols]
    block_terms = jnp.einsum("kij,kjf->kif", tile_edges, picked, precision=precise)
    partial_sum = jnp.einsum("dk,kif->dif", dest_select, block_terms, precision=precise)
    summed = lax.psum_scatter(
        partial_sum.reshape(grid_rows * row_count, feat_width),
        "row",
        scatter_dimension=0,
        tiled=True,
    )
    activated, pullback = jax.vjp(activate, summed)
    (grad_pre,) = pullback(cotangent)
    grad_scale = float(row_count * grid_rows * col_count) ** (-0.5)
    gathered = lax.all_gather(grad_pre, "row", axis=0, tiled=True)
    dest_rows = gathered.reshape(dest_blocks, block_size, feat_width)[tile_rows]
    back_terms = jnp.einsum("kji,kjf->kif", tile_edges, dest_rows, precision=precise)
    slot_grad = jnp.einsum("sk,kif->sif", source_select, back_terms, precision=precise)
    returned = lax.all_to_all(
        slot_grad.reshape(col_count, capacity, feat_width),
        "col",
        split_axis=0,
        concat_axis=0,
        tiled=True,
    )
    node_grad = returned.reshape(col_count * capacity, feat_width)[slot_index]
    input_grad = jnp.dot(node_grad, weight.T, precision=precise, preferred_element_type=jnp.float32)
    local_weight = (
        jnp.dot(features.T, node_grad, precision=precise, preferred_element_type=jnp.float32)
        * grad_scale
    )
    weight_grad = lax.psum(local_weight, ("row", "col"))
    return (activated, input_grad, weight_grad)


def solution(mesh):
    placed = (
        P(("groups", "row", "col"), None),
        P(),
        P(("groups", "row", "col"), None),
        P(("groups", "row", "col"), None),
        P(("groups", "row", "col"), None),
        P(("groups", "row", "col"), None),
        P(("groups", "row", "col"), None, None, None),
    )
    return jax.shard_map(
        local,
        mesh=mesh,
        in_specs=placed,
        out_specs=(
            P(("groups", "row", "col"), None),
            P(("groups", "row", "col"), None),
            P("groups", None),
        ),
        check_vma=False,
    )
```

profile of v0, /device:TPU:1, one launch (start us, length us, event | category | flops | bytes accessed | tf_op | source)
XLA Modules:
  0.0 285.8 jit_solution(17520739598416967375)
XLA Ops:
  11.1 1.7 fusion.29
  12.8 3.3 %scatter_custom_fusion = f32[1024,256]{1,0:T(8,128)} fusion(s32[512]{0:T(512)S(1)} %bitcast.74, f32[512,256]{1,0:T(8,128)S(1)} %fusion.29, f32[]{:T(128)} %constant.13.clone.1), kind=kCustom, calls=%fused_computation.22 | custom fusion | bytes 1048580 | tf_op jit(solution)/shard_map/scatter | solution.py:35
  16.1 5.4 %all-to-all-start = ((f32[4,256,256]{2,1,0:T(8,128)}), f32[4,256,256]{2,1,0:T(8,128)S(1)}, u32[]{:S(2)}, u32[]{:S(2)}) async-start(f32[4,256,256]{2,1,0:T(8,128)} %bitcast.70), calls=%async_computation | async-start | bytes 2097152 | tf_op jit(solution)/shard_map/all_to_all | solution.py:36
  21.5 25.2 %all-to-all-done = f32[4,256,256]{2,1,0:T(8,128)S(1)} async-done(((f32[4,256,256]{2,1,0:T(8,128)}), f32[4,256,256]{2,1,0:T(8,128)S(1)}, u32[]{:S(2)}, u32[]{:S(2)}) %all-to-all-start) | async-done | bytes 1048608 | tf_op jit(solution)/shard_map/all_to_all | solution.py:36
  46.7 2.8 gather_fusion
  49.5 10.4 %fusion.6 = f32[32,256,128]{2,1,0:T(8,128)} fusion(f32[32,128,256]{2,1,0:T(8,128)} %gather_fusion, f32[1,32,128,128]{3,2,1,0:T(8,128)S(1)} %copy-done), kind=kOutput, calls=%fused_computation.10 | convolution fusion | flops 1610612736 | bytes 10485760 | tf_op jit(solution)/shard_map/kij,kjf->kif/dot_general | solution.py:45
  59.9 5.5 %copy.14 = f32[32,256,128]{1,0,2:T(8,128)} copy(f32[32,256,128]{2,1,0:T(8,128)} %fusion.6) | data formatting | bytes 8388608 | tf_op jit(solution)/shard_map/kij,kjf->kif/dot_general | solution.py:45
  65.4 3.8 %fusion.2 = f32[16,128,256]{2,0,1:T(8,128)S(1)} fusion(f32[32,256,128]{1,0,2:T(8,128)} %copy.14, s32[32]{0:T(128)S(1)} %bitcast.78), kind=kOutput, calls=%fused_computation.6 | convolution fusion | flops 201327104 | bytes 6291584 | tf_op jit(solution)/shard_map/dk,kif->dif/dot_general | solution.py:46
  69.2 2.6 copy.11
  72.0 31.2 %reduce-scatter.2.cloned.1.call-done = f32[512,256]{1,0:T(8,128)} async-done(((f32[2048,256]{1,0:T(8,128)}), f32[512,256]{1,0:T(8,128)}) %reduce-scatter.2.cloned.1.call-update) | async-done | bytes 524304 | tf_op jit(solution)/shard_map/reduce_scatter | solution.py:47
  103.3 2.4 fusion.14
  105.7 23.1 %all-gather.2.cloned.1.call-done = f32[2048,256]{1,0:T(8,128)} async-done(((f32[512,256]{1,0:T(8,128)}), f32[2048,256]{1,0:T(8,128)}) %all-gather.2.cloned.1.call-update) | async-done | bytes 2097168 | tf_op jit(solution)/shard_map/all_gather | solution.py:56
  128.8 4.3 %gather_fusion.1 = f32[32,128,256]{2,1,0:T(8,128)} fusion(f32[16,128,256]{2,1,0:T(8,128)} %bitcast.68, s32[1024]{0:T(1024)S(1)} %pad_clamp_fusion.1), kind=kCustom, calls=%fused_computation.1 | custom fusion | bytes 8388736 | tf_op jit(solution)/shard_map/gather | solution.py:57
  133.1 10.4 %fusion.4 = f32[32,256,128]{2,1,0:T(8,128)} fusion(f32[32,128,256]{2,1,0:T(8,128)} %gather_fusion.1, f32[1,32,128,128]{3,2,1,0:T(8,128)S(1)} %copy-done), kind=kOutput, calls=%fused_computation.8 | convolution fusion | flops 1610612736 | bytes 10485760 | tf_op jit(solution)/shard_map/kji,kjf->kif/dot_general | solution.py:58
  143.6 5.5 %copy.15 = f32[32,256,128]{1,0,2:T(8,128)} copy(f32[32,256,128]{2,1,0:T(8,128)} %fusion.4) | data formatting | bytes 8388608 | tf_op jit(solution)/shard_map/kji,kjf->kif/dot_general | solution.py:58
  149.1 3.6 %fusion = f32[8,128,256]{2,0,1:T(8,128)S(1)} fusion(f32[32,256,128]{1,0,2:T(8,128)} %copy.15, s32[32]{0:T(128)S(1)} %bitcast.79), kind=kOutput, calls=%fused_computation.4 | convolution fusion | flops 100663552 | bytes 5243008 | tf_op jit(solution)/shard_map/sk,kif->sif/dot_general | solution.py:59
  152.7 1.3 copy.12
  154.0 4.5 %all-to-all-start.1 = ((f32[4,256,256]{2,1,0:T(8,128)}), f32[4,256,256]{2,1,0:T(8,128)S(1)}, u32[]{:S(2)}, u32[]{:S(2)}) async-start(f32[4,256,256]{2,1,0:T(8,128)} %bitcast.71), calls=%async_computation.2 | async-start | bytes 2097152 | tf_op jit(solution)/shard_map/all_to_all | solution.py:60
  158.5 25.3 %all-to-all-done.1 = f32[4,256,256]{2,1,0:T(8,128)S(1)} async-done(((f32[4,256,256]{2,1,0:T(8,128)}), f32[4,256,256]{2,1,0:T(8,128)S(1)}, u32[]{:S(2)}, u32[]{:S(2)}) %all-to-all-start.1) | async-done | bytes 1048608 | tf_op jit(solution)/shard_map/all_to_all | solution.py:60
  183.8 2.2 gather_fusion.2
  186.0 2.9 %fusion.8 = f32[256,256]{0,1:T(8,128)} fusion(f32[512,256]{1,0:T(8,128)} %gather_fusion.2, f32[512,256]{1,0:T(8,128)} %param.7), kind=kOutput, calls=%fused_computation.13 | convolution fusion | flops 402718720 | bytes 1310720 | tf_op jit(solution)/shard_map/dot_general | solution.py:70
  188.9 2.5 fusion.30
  191.4 86.1 %all-reduce.2.cloned.1.call-done = f32[256,256]{0,1:T(8,128)} async-done(((f32[256,256]{0,1:T(8,128)}), f32[256,256]{0,1:T(8,128)}) %all-reduce.2.cloned.1.call-update) | async-done | bytes 262160 | tf_op jit(solution)/shard_map/psum | solution.py:73
  277.5 1.8 copy.13
  (28 shorter events, 4.2 us)
Async XLA Ops:
  7.2 42.3 %copy-start = (f32[1,32,128,128]{3,2,1,0:T(8,128)S(1)}, f32[1,32,128,128]{3,2,1,0:T(8,128)}, u32[]{:S(2)}) copy-start(f32[1,32,128,128]{3,2,1,0:T(8,128)} %param.13) | copy-start | bytes 6291460
  7.2 14.3 %copy-start.4 = (s32[1,32]{1,0:T(1,128)S(1)}, s32[1,32]{1,0:T(1,128)}, u32[]{:S(2)}) copy-start(s32[1,32]{1,0:T(1,128)} %param.12) | copy-start | bytes 388
  16.1 30.7 %all-to-all-start = ((f32[4,256,256]{2,1,0:T(8,128)}), f32[4,256,256]{2,1,0:T(8,128)S(1)}, u32[]{:S(2)}, u32[]{:S(2)}) async-start(f32[4,256,256]{2,1,0:T(8,128)} %bitcast.70), calls=%async_computation | async-start | bytes 2097152 | tf_op jit(solution)/shard_map/all_to_all | solution.py:36
  21.5 81.8 %reduce-scatter.2.cloned.1.call-start = ((), (), s32[]{:S(2)}) async-start(), calls=%async_computation.3 | async-start | bytes 2621440 | tf_op jit(solution)/shard_map/reduce_scatter | solution.py:47
  59.9 5.5 %copy-start.3 = (s32[1,32]{1,0:T(1,128)S(1)}, s32[1,32]{1,0:T(1,128)}, u32[]{:S(2)}) copy-start(s32[1,32]{1,0:T(1,128)} %param.11) | copy-start | bytes 388
  69.2 34.1 %copy-start.2 = (f32[512,256]{1,0:T(8,128)S(1)}, f32[512,256]{1,0:T(8,128)}, u32[]{:S(2)}) copy-start(f32[512,256]{1,0:T(8,128)} %param.9) | copy-start | bytes 1572868
  71.8 57.0 %all-gather.2.cloned.1.call-start = ((), (), s32[]{:S(2)}) async-start(), calls=%async_computation.4 | async-start | bytes 2621440 | tf_op jit(solution)/shard_map/all_gather | solution.py:56
  154.0 34.9 %copy-start.1 = (f32[256,256]{1,0:T(8,128)S(1)}, f32[256,256]{1,0:T(8,128)}, u32[]{:S(2)}) copy-start(f32[256,256]{1,0:T(8,128)} %param.8) | copy-start | bytes 786436
  154.0 29.7 %all-to-all-start.1 = ((f32[4,256,256]{2,1,0:T(8,128)}), f32[4,256,256]{2,1,0:T(8,128)S(1)}, u32[]{:S(2)}, u32[]{:S(2)}) async-start(f32[4,256,256]{2,1,0:T(8,128)} %bitcast.71), calls=%async_computation.2 | async-start | bytes 2097152 | tf_op jit(solution)/shard_map/all_to_all | solution.py:60
  158.5 119.0 %all-reduce.2.cloned.1.call-start = ((), (), s32[]{:S(2)}) async-start(), calls=%async_computation.5 | async-start | bytes 524288 | tf_op jit(solution)/shard_map/psum | solution.py:73
Sparse Core Ops, SparseCore 0:
  71.9 31.2 reduce-scatter.1
  105.8 22.9 all-gather.1
  189.0 88.3 all-reduce.1
where the time goes:
time: 287 us; the launch traced here: 286 us
  waiting for transfers between devices  191 us (67%)
  matrix products  35.3 us (12%)
  local copies, waits for them, and re-layouts  29.5 us (10%)
  between operations  13.8 us (5%)
  starting transfers between devices  10.1 us (4%)
  other arithmetic  6.09 us (2%)
    psum x1, waiting for transfers between devices, local(): weight_grad = lax.psum(local_weight, ('row', 'col'))  86.1 us
    reduce_scatter x1, waiting for transfers between devices, local(): lax.psum_scatter(partial_sum.reshape(grid_rows * row_count, feat_width),...  31.2 us
    all_to_all x1, waiting for transfers between devices, local(): lax.all_to_all(slot_grad.reshape(col_count, capacity, feat_width), 'col',...  25.3 us
    all_to_all x1, waiting for transfers between devices, local(): lax.all_to_all(buffer.reshape(col_count, capacity, feat_width), 'col', sp...  25.2 us
    all_gather x1, waiting for transfers between devices, local(): gathered = lax.all_gather(grad_pre, 'row', axis=0, tiled=True)  23.1 us
    dot_general x1, matrix products, local(): jnp.einsum('kji,kjf->kif', tile_edges, dest_rows, precision=precise)  10.4 us
    dot_general x1, matrix products, local(): jnp.einsum('kij,kjf->kif', tile_edges, picked, precision=precise)  10.4 us
  transfers between devices with their start and end apart: 5, of which 5 were waited for; matrix products, arithmetic and copies ran while one was open for 1% of the time, Pallas kernels for 0%

commit v1 on v0

v1 whole, which is shorter than its diff:
```python
import functools
import math

import jax
import jax.numpy as jnp
from jax import lax
from jax.experimental import pallas as pl
from jax.experimental.pallas import tpu as pltpu
from jax.sharding import PartitionSpec as P

MESH = pl.DeviceIdType.MESH
F32, BF16, I32 = jnp.float32, jnp.bfloat16, jnp.int32
PARTS = 2


def split(value):
    high = value.astype(BF16)
    return high, (value - high.astype(F32)).astype(BF16)


def wide(value):
    return jnp.concatenate(split(value), axis=1)


def mm(a, b, dims=((1,), (0,))):
    return lax.dot_general(a, b, (dims, ((), ())), preferred_element_type=F32)


def mm3(a, b, dims=((1,), (0,))):
    return mm(a[0], b[0], dims) + mm(a[1], b[0], dims) + mm(a[0], b[1], dims)


def each(start, stop, body):
    if stop - start <= 8:
        for i in range(start, stop):
            body(i)
    else:

        def step(i, carry):
            body(i)
            return carry

        lax.fori_loop(start, stop, step, 0)


def order_of(own, other, meta, base):
    count = own.shape[1]
    row_at = lax.broadcasted_iota(I32, (count, count), 0)
    lane_at = lax.broadcasted_iota(I32, (count, count), 1)

    def upright(v):
        return jnp.sum(jnp.where(row_at == lane_at, jnp.broadcast_to(v, row_at.shape), 0), axis=1, keepdims=True)

    own_up, other_up = upright(own), upright(other)
    before = (own < own_up) | ((own == own_up) & (lane_at < row_at))
    rank = jnp.sum(before.astype(I32), axis=1, keepdims=True)
    placed = rank == lane_at

    def lay(v):
        return jnp.sum(jnp.where(placed, v, 0), axis=0, keepdims=True)

    meta[base : base + 1, :count] = lay(row_at)
    meta[base + 1 : base + 2, :count] = lay(jnp.broadcast_to(own_up, row_at.shape))
    meta[base + 2 : base + 3, :count] = lay(jnp.broadcast_to(other_up, row_at.shape))
    meta[base + 3 : base + 4, :count] = jnp.maximum(
        jnp.sum((own_up <= lane_at).astype(I32), axis=0, keepdims=True) - 1, 0
    )
    meta[base + 4 : base + 5, :count] = jnp.sum((own_up == lane_at).astype(I32), axis=0, keepdims=True)


def kernel(
    sizes,
    features_hbm, weight_ref, cotangent_hbm, column_ref, rows_ref, cols_ref, edges_hbm,
    activated_ref, input_ref, wgrad_ref,
    feat, cot, edges, edge_f, edge_b, meta, plan, onehot, onehot_t,
    send, recv, table, run, dest, near, mid, far, agg, every, back, back_in,
    wpart, wrow, wsum, wcol, wown, wall,
    load_sem, a_send, a_recv, n_send, n_recv, g_send, g_recv, b_send, b_recv,
    wr_send, wr_recv, wz_send, wz_recv, wy_send, wy_recv, wx_send, wx_recv,
):
    n_row, n_col, cap, block, d_blocks, s_blocks, reducers = sizes
    count = edges.shape[0]
    rd, width = feat.shape
    half = width // PARTS
    row, col = lax.axis_index("row"), lax.axis_index("col")
    p1 = row + 1 - 2 * lax.rem(row, 2)
    p2 = lax.rem(row + 2, n_row)
    p3 = lax.rem(p1 + 2, n_row)

    def remote(src, dst, s_sem, r_sem, where):
        return pltpu.make_async_remote_copy(
            src_ref=src, dst_ref=dst, send_sem=s_sem, recv_sem=r_sem, device_id=where, device_id_type=MESH
        )

    barrier = pltpu.get_barrier_semaphore()
    each(1, n_row, lambda k: pl.semaphore_signal(
        barrier, inc=1, device_id={"row": lax.rem(row + k, n_row)}, device_id_type=MESH))
    each(1, n_col, lambda k: pl.semaphore_signal(
        barrier, inc=1, device_id={"col": lax.rem(col + k, n_col)}, device_id_type=MESH))

    load_f = pltpu.make_async_copy(features_hbm, feat, load_sem.at[0])
    load_e = pltpu.make_async_copy(edges_hbm, edges, load_sem.at[1])
    load_c = pltpu.make_async_copy(cotangent_hbm, cot, load_sem.at[2])
    load_f.start()
    load_e.start()
    load_c.start()

    target = column_ref[...]
    named = lax.broadcasted_iota(I32, (rd, 128), 1) == target
    below = lax.broadcasted_iota(I32, (rd, rd), 1) < lax.broadcasted_iota(I32, (rd, rd), 0)
    earlier = mm(below.astype(F32).astype(BF16), named.astype(F32).astype(BF16))
    rank = jnp.sum(jnp.where(named, earlier, 0.0), axis=1, keepdims=True)
    slot = target * cap + rank.astype(I32)
    same = lax.broadcasted_iota(I32, (rd, rd), 1) == lax.broadcasted_iota(I32, (rd, rd), 0)
    slot_row = jnp.sum(jnp.where(same, jnp.broadcast_to(slot, (rd, rd)), 0), axis=0, keepdims=True)
    slots = n_col * cap
    onehot[...] = (lax.broadcasted_iota(I32, (slots, rd), 0) == slot_row).astype(F32).astype(BF16)
    load_f.wait()

    def route_copy(part, k):
        to = lax.rem(col + k, n_col)
        return remote(
            send.at[part, pl.ds(pl.multiple_of(to * cap, cap), cap)],
            recv.at[part, pl.ds(pl.multiple_of(col * cap, cap), cap)],
            a_send.at[part, to], a_recv.at[part, col], {"col": to},
        )

    def route_arrival(part, k):
        of = lax.rem(col + k, n_col)
        return remote(
            send.at[part, pl.ds(pl.multiple_of(of * cap, cap), cap)],
            recv.at[part, pl.ds(pl.multiple_of(of * cap, cap), cap)],
            a_send.at[part, of], a_recv.at[part, of], {"col": of},
        )

    mine = pl.ds(pl.multiple_of(col * cap, cap), cap)
    for part in range(PARTS):
        both = mm(onehot[...], wide(feat[:, part * half : (part + 1) * half]))
        send[part] = both[:, :half] + both[:, half:]
        if part == 0:
            pl.semaphore_wait(barrier, n_row + n_col - 2)
        each(1, n_col, lambda k: route_copy(part, k).start())
        recv[part, mine] = send[part, mine]

    order_of(rows_ref[...], cols_ref[...], meta, 0)
    order_of(cols_ref[...], rows_ref[...], meta, 8)
    load_m = pltpu.make_async_copy(meta, plan, load_sem.at[3])
    load_m.start()
    onehot_t[...] = (lax.broadcasted_iota(I32, (rd, slots), 1) == slot).astype(F32).astype(BF16)
    load_e.wait()

    def prepare(k, carry):
        value = edges[k]
        edge_f[k] = wide(value)
        edge_b[k] = wide(value.T)
        return carry

    lax.fori_loop(0, count, prepare, 0)
    load_m.wait()
    load_c.wait()
    w_pair = split(weight_ref[...])

    def fill(at, value):
        pair = wide(value)
        table[at, :block] = pair
        table[at, block:] = pair

    def multiply(edge_ref, base):
        def step(p, total):
            product = mm(edge_ref[plan[base, p]], table[plan[base + 2, p]])
            kept = plan[base + 1, p] == plan[base + 1, jnp.maximum(p - 1, 0)]
            total = jnp.where(kept, total, 0.0) + product[:, :half] + product[:, half:]
            run[p] = total
            return total

        lax.fori_loop(0, count, step, jnp.zeros((block, half), F32), unroll=8)

    def taken(base, at):
        return jnp.where(plan[base + 4, at] > 0, run[plan[base + 3, at]], 0.0)

    per = rd // block

    def near_copy(part, which):
        return remote(
            dest.at[part, p3 if which == 0 else p1], near.at[part, which],
            n_send.at[part, which], n_recv.at[part, which], {"row": p1},
        )

    def far_copy(part):
        return remote(mid.at[part], far.at[part], n_send.at[part, 2], n_recv.at[part, 2], {"row": p2})

    for part in range(PARTS):
        each(1, n_col, lambda k: route_arrival(part, k).wait_recv())
        for s in range(s_blocks):
            fill(s, recv[part, s * block : (s + 1) * block])
        multiply(edge_f, 0)
        for which, owner in enumerate((p3, p1, p2, row)):
            for i in range(per):
                dest[part, owner, i * block : (i + 1) * block] = taken(0, owner * per + i)
            if which < 2:
                near_copy(part, which).start()
        near_copy(part, 0).wait_recv()
        mid[part] = dest[part, p2] + near[part, 0]
        far_copy(part).start()

    for part in range(PARTS):
        near_copy(part, 1).wait_recv()
        far_copy(part).wait_recv()
        agg[:, part * half : (part + 1) * half] = dest[part, row] + near[part, 1] + far[part]

    agg_pair = split(agg[...])
    x = mm3(agg_pair, w_pair)
    scale = math.sqrt(2.0 / math.pi)
    square = x * x
    t = jnp.tanh(scale * (x + 0.044715 * (square * x)))
    activated_ref[...] = 0.5 * x * (1.0 + t)
    slope = 0.5 * (1.0 + t) + 0.5 * x * (1.0 - t * t) * (scale * (1.0 + 3.0 * 0.044715 * square))
    grad_pair = split(cot[...] * slope)
    grad = mm3(grad_pair, w_pair, ((1,), (1,)))

    def give(part, which):
        at = row if which < 2 else p2
        return remote(
            every.at[part, at], every.at[part, at],
            g_send.at[part, which], g_recv.at[part, which], {"row": p2 if which == 0 else p1},
        )

    def take(part, which):
        at = (p2, p1, p3)[which]
        return remote(
            every.at[part, at], every.at[part, at],
            g_send.at[part, which], g_recv.at[part, which], {"row": p2 if which == 0 else p1},
        )

    piece = width // n_row

    def w_row_copy(k):
        to = lax.rem(row + k, n_row)
        return remote(wpart.at[to], wrow.at[row], wr_send.at[to], wr_recv.at[row], {"row": to})

    def w_row_arrival(k):
        of = lax.rem(row + k, n_row)
        return remote(wpart.at[of], wrow.at[of], wr_send.at[of], wr_recv.at[of], {"row": of})

    for part in range(PARTS):
        every[part, row] = grad[:, part * half : (part + 1) * half]
        give(part, 0).start()
        give(part, 1).start()
        if part == 0:
            wlocal = mm3(agg_pair, grad_pair, ((0,), (0,)))
            for r in range(n_row):
                wpart[r] = wlocal[r * piece : (r + 1) * piece]
            each(1, n_row, lambda k: w_row_copy(k).start())

    def back_copy(part, k):
        to = lax.rem(col + k, n_col)
        return remote(
            back.at[part, pl.ds(pl.multiple_of(to * cap, cap), cap)],
            back_in.at[part, pl.ds(pl.multiple_of(col * cap, cap), cap)],
            b_send.at[part, to], b_recv.at[part, col], {"col": to},
        )

    def back_arrival(part, k):
        of = lax.rem(col + k, n_col)
        return remote(
            back.at[part, pl.ds(pl.multiple_of(of * cap, cap), cap)],
            back_in.at[part, pl.ds(pl.multiple_of(of * cap, cap), cap)],
            b_send.at[part, of], b_recv.at[part, of], {"col": of},
        )

    share = piece // reducers

    def w_col_copy(to):
        return remote(wsum.at[to], wcol.at[col], wz_send.at[to], wz_recv.at[col], {"col": to})

    def w_col_arrival(of):
        return remote(wsum.at[0], wcol.at[of], wz_send.at[0], wz_recv.at[of], {"col": of})

    def w_col_give(k):
        to = lax.rem(col + k, n_col)
        return remote(wown, wall.at[row, col], wy_send.at[to], wy_recv.at[col], {"col": to})

    def w_col_take(of):
        return remote(wown, wall.at[row, of], wy_send.at[of], wy_recv.at[of], {"col": of})

    def w_row_give(k):
        to = lax.rem(row + k, n_row)
        return remote(wall.at[row], wall.at[row], wx_send.at[to], wx_recv.at[row], {"row": to})

    def w_row_take(k):
        of = lax.rem(row + k, n_row)
        return remote(wall.at[of], wall.at[of], wx_send.at[of], wx_recv.at[of], {"row": of})

    def reducer(body):
        if reducers == n_col:
            body()
        else:
            pl.when(col < reducers)(body)

    def others(of, body):
        pl.when(of != col)(body)

    def w_second():
        each(1, n_row, lambda k: w_row_arrival(k).wait_recv())
        total = wpart[row]
        for k in range(1, n_row):
            total = total + wrow[lax.rem(row + k, n_row)]
        for j in range(reducers):
            wsum[j] = total[j * share : (j + 1) * share]
        if reducers == n_col:
            each(1, n_col, lambda k: w_col_copy(lax.rem(col + k, n_col)).start())
        else:
            each(0, reducers, lambda j: others(j, lambda: w_col_copy(j).start()))

    def w_third():
        def body():
            each(1, n_col, lambda k: w_col_arrival(lax.rem(col + k, n_col)).wait_recv())
            wcol[col] = wsum[col]
            total = wcol[0]
            for j in range(1, n_col):
                total = total + wcol[j]
            wown[...] = total * (float(rd * n_row * n_col) ** -0.5)
            each(1, n_col, lambda k: w_col_give(k).start())
            wall[row, col] = wown[...]

        reducer(body)

    def w_fourth():
        if reducers == n_col:
            each(1, n_col, lambda k: w_col_take(lax.rem(col + k, n_col)).wait_recv())
        else:
            each(0, reducers, lambda j: others(j, lambda: w_col_take(j).wait_recv()))
        each(1, n_row, lambda k: w_row_give(k).start())

    for part in range(PARTS):
        take(part, 0).wait_recv()
        give(part, 2).start()
        take(part, 1).wait_recv()
        take(part, 2).wait_recv()
        for owner in range(n_row):
            for i in range(per):
                fill(owner * per + i, every[part, owner, i * block : (i + 1) * block])
        multiply(edge_b, 8)
        for s in range(s_blocks):
            back[part, s * block : (s + 1) * block] = taken(8, s)
        each(1, n_col, lambda k: back_copy(part, k).start())
        back_in[part, mine] = back[part, mine]
        if part == 0:
            w_second()
        else:
            w_third()

    for part in range(PARTS):
        each(1, n_col, lambda k: back_arrival(part, k).wait_recv())
        both = mm(onehot_t[...], wide(back_in[part]))
        input_ref[:, part * half : (part + 1) * half] = both[:, :half] + both[:, half:]
        if part == 0:
            w_fourth()
    each(1, n_row, lambda k: w_row_take(k).wait_recv())
    for r in range(n_row):
        for j in range(reducers):
            wgrad_ref[r * piece + j * share : r * piece + (j + 1) * share] = wall[r, j]

    for part in range(PARTS):
        each(1, n_col, lambda k: route_copy(part, k).wait_send())
        each(1, n_col, lambda k: back_copy(part, k).wait_send())
        near_copy(part, 0).wait_send()
        near_copy(part, 1).wait_send()
        far_copy(part).wait_send()
        for which in range(3):
            give(part, which).wait_send()
    each(1, n_row, lambda k: w_row_copy(k).wait_send())
    each(1, n_row, lambda k: w_row_give(k).wait_send())
    if reducers == n_col:
        each(1, n_col, lambda k: w_col_copy(lax.rem(col + k, n_col)).wait_send())
    else:
        each(0, reducers, lambda j: others(j, lambda: w_col_copy(j).wait_send()))
    reducer(lambda: each(1, n_col, lambda k: w_col_give(k).wait_send()))


def local(n_row, n_col, features, weight, cotangent, column_of, block_rows, block_cols, edge_blocks):
    rd, width = features.shape
    count, block = edge_blocks.shape[1:3]
    cap = max(2, 2 * rd // n_col)
    slots = n_col * cap
    d_blocks, s_blocks = n_row * rd // block, slots // block
    half = width // PARTS
    piece = width // n_row
    reducers = min(n_col, piece // 8)
    share = piece // reducers
    sizes = (n_row, n_col, cap, block, d_blocks, s_blocks, reducers)
    vmem = pl.BlockSpec(memory_space=pltpu.VMEM)
    hbm = pl.BlockSpec(memory_space=pl.ANY)
    V, D = pltpu.VMEM, pltpu.SemaphoreType.DMA
    return pl.pallas_call(
        functools.partial(kernel, sizes),
        out_shape=(
            jax.ShapeDtypeStruct((rd, width), F32),
            jax.ShapeDtypeStruct((rd, width), F32),
            jax.ShapeDtypeStruct((width, width), F32),
        ),
        in_specs=[hbm, vmem, hbm, vmem, vmem, vmem, hbm],
        out_specs=(vmem, vmem, vmem),
        scratch_shapes=[
            V((rd, width), F32),
            V((rd, width), F32),
            V((count, block, block), F32),
            V((count, block, 2 * block), BF16),
            V((count, block, 2 * block), BF16),
            V((16, 128), I32),
            pltpu.SMEM((16, 128), I32),
            V((slots, rd), BF16),
            V((rd, slots), BF16),
            V((PARTS, slots, half), F32),
            V((PARTS, slots, half), F32),
            V((max(d_blocks, s_blocks), 2 * block, 2 * half), BF16),
            V((count, block, half), F32),
            V((PARTS, n_row, rd, half), F32),
            V((PARTS, 2, rd, half), F32),
            V((PARTS, rd, half), F32),
            V((PARTS, rd, half), F32),
            V((rd, width), F32),
            V((PARTS, n_row, rd, half), F32),
            V((PARTS, slots, half), F32),
            V((PARTS, slots, half), F32),
            V((n_row, piece, width), F32),
            V((n_row, piece, width), F32),
            V((reducers, share, width), F32),
            V((n_col, share, width), F32),
            V((share, width), F32),
            V((n_row, reducers, share, width), F32),
            D((4,)),
            D((PARTS, n_col)), D((PARTS, n_col)),
            D((PARTS, 3)), D((PARTS, 3)),
            D((PARTS, 3)), D((PARTS, 3)),
            D((PARTS, n_col)), D((PARTS, n_col)),
            D((n_row,)), D((n_row,)),
            D((n_col,)), D((n_col,)),
            D((n_col,)), D((n_col,)),
            D((n_row,)), D((n_row,)),
        ],
        compiler_params=pltpu.CompilerParams(
            collective_id=0, has_side_effects=True, vmem_limit_bytes=48 * 2**20
        ),
    )(features, weight, cotangent, column_of, block_rows, block_cols, edge_blocks[0])


def solution(mesh):
    spread = P(("groups", "row", "col"), None)
    placed = (spread, P(), spread, spread, spread, spread, P(("groups", "row", "col"), None, None, None))
    return jax.shard_map(
        functools.partial(local, mesh.shape["row"], mesh.shape["col"]),
        mesh=mesh,
        in_specs=placed,
        out_specs=(spread, spread, P("groups", None)),
        check_vma=False,
    )
```

time: 287 us -> 91.1 us (0.32)
  waiting for transfers between devices: 191 us -> 0 us
  Pallas kernels: 0 us -> 80.3 us
  matrix products: 35.3 us -> 0 us
  local copies, waits for them, and re-layouts: 29.5 us -> 9.04 us
  between operations: 13.8 us -> 0.66 us
  starting transfers between devices: 10.1 us -> 0 us
  other arithmetic: 6.09 us -> 0 us
    psum x1 -> x0, waiting for transfers between devices: 86.1 us -> none  [local(): weight_grad = lax.psum(local_weight, ('row', 'col'))]
    pallas_call x0 -> x1, Pallas kernels: none -> 80.3 us  [local(): pl.pallas_call(functools.partial(kernel, sizes), out_shape=(jax.ShapeDtyp...]
    all_to_all x2 -> x0, waiting for transfers between devices: 50.5 us -> none  [the longest x1 25.3 us: local(): lax.all_to_all(slot_grad.reshape(col_count, capacity, feat_width), 'col',...]
    dot_general x7 -> x0, matrix products: 35.3 us -> none  [the longest x1 10.4 us: local(): jnp.einsum('kji,kjf->kif', tile_edges, dest_rows, precision=precise)]
    reduce_scatter x1 -> x0, waiting for transfers between devices: 31.2 us -> none  [local(): lax.psum_scatter(partial_sum.reshape(grid_rows * row_count, feat_width),...]
    all_gather x1 -> x0, waiting for transfers between devices: 23.1 us -> none  [local(): gathered = lax.all_gather(grad_pre, 'row', axis=0, tiled=True)]
    dot_general x4 -> x0, local copies, waits for them, and re-layouts: 14.9 us -> none  [the longest x1 5.51 us: local(): jnp.einsum('kij,kjf->kif', tile_edges, picked, precision=precise)]
    all_to_all x2 -> x0, starting transfers between devices: 9.88 us -> none  [the longest x1 5.42 us: local(): lax.all_to_all(buffer.reshape(col_count, capacity, feat_width), 'col', sp...]
  transfers between devices with their start and end apart: 5 -> 0, of which waited for: 5 -> 0; matrix products, arithmetic and copies ran while one was open for 1% -> 0% of each run, Pallas kernels for 0% -> 0%
where the time goes in v1:
time: 91.1 us; the launch traced here: 90 us
  Pallas kernels  80.3 us (88%)
  local copies, waits for them, and re-layouts  9.04 us (10%)
    pallas_call x1, Pallas kernels, local(): pl.pallas_call(functools.partial(kernel, sizes), out_shape=(jax.ShapeDtyp...  80.3 us
    unnamed x16, local copies, waits for them, and re-layouts  9.04 us

profile of v1, /device:TPU:1, one launch (start us, length us, event | category | flops | bytes accessed | tf_op | source)
XLA Modules:
  0.0 90.0 jit_solution(15389768142203574526)
XLA Ops:
  0.6 0.8 copy.10.column_ref
  1.5 0.0 copy-start
  1.5 1.6 %copy-done = f32[1,32,128,128]{3,2,1,0:T(8,128)S(1)} copy-done((f32[1,32,128,128]{3,2,1,0:T(8,128)S(1)}, f32[1,32,128,128]{3,2,1,0:T(8,128)}, u32[]{:S(2)}) %copy-start) | copy-done | bytes 2097176
  3.1 0.0 copy-start.1
  3.1 1.0 %copy-done.1 = f32[512,256]{1,0:T(8,128)S(1)} copy-done((f32[512,256]{1,0:T(8,128)S(1)}, f32[512,256]{1,0:T(8,128)}, u32[]{:S(2)}) %copy-start.1) | copy-done | bytes 524312
  4.1 0.0 copy-start.2
  4.1 1.0 %copy-done.2 = f32[512,256]{1,0:T(8,128)S(1)} copy-done((f32[512,256]{1,0:T(8,128)S(1)}, f32[512,256]{1,0:T(8,128)}, u32[]{:S(2)}) %copy-start.2) | copy-done | bytes 524312
  5.1 0.0 copy-start.3
  5.1 0.9 %copy-done.3 = f32[256,256]{1,0:T(8,128)S(1)} copy-done((f32[256,256]{1,0:T(8,128)S(1)}, f32[256,256]{1,0:T(8,128)}, u32[]{:S(2)}) %copy-start.3) | copy-done | bytes 262168
  6.1 0.0 copy-start.4
  6.1 0.7 copy-done.4
  6.7 0.0 copy-start.5
  6.7 0.7 copy-done.5
  7.4 80.3 %shard_map.94 = (f32[512,256]{1,0:T(8,128)S(1)}, f32[512,256]{1,0:T(8,128)S(1)}, f32[256,256]{1,0:T(8,128)S(1)}) custom-call(f32[512,256]{1,0:T(8,128)S(1)} %copy-done.1, f32[256,256]{1,0:T(8,128)S(1)} %copy-done.3, f32[512,256]{1,0:T(8,128)S(1)} %copy-done.2, s32[512,1]{1,0:T(8,128)S(1)} %copy.10.column_ref, s32[1,32]{1,0:T(1,128)S(1)} %copy-done.4, ...), custom_call_target="tpu_custom_call" | custom-call | tf_op jit(solution)/shard_map/pallas_call | solution.py:395
  87.7 0.8 copy.14
  88.5 0.8 copy.15
  89.3 0.7 copy.16
Async XLA Ops:
  1.5 1.6 %copy-start = (f32[1,32,128,128]{3,2,1,0:T(8,128)S(1)}, f32[1,32,128,128]{3,2,1,0:T(8,128)}, u32[]{:S(2)}) copy-start(f32[1,32,128,128]{3,2,1,0:T(8,128)} %param.13) | copy-start | bytes 6291460
  3.1 1.0 %copy-start.1 = (f32[512,256]{1,0:T(8,128)S(1)}, f32[512,256]{1,0:T(8,128)}, u32[]{:S(2)}) copy-start(f32[512,256]{1,0:T(8,128)} %features_hbm.1) | copy-start | bytes 1572868
  4.1 1.0 %copy-start.2 = (f32[512,256]{1,0:T(8,128)S(1)}, f32[512,256]{1,0:T(8,128)}, u32[]{:S(2)}) copy-start(f32[512,256]{1,0:T(8,128)} %cotangent_hbm.1) | copy-start | bytes 1572868
  5.1 0.9 %copy-start.3 = (f32[256,256]{1,0:T(8,128)S(1)}, f32[256,256]{1,0:T(8,128)}, u32[]{:S(2)}) copy-start(f32[256,256]{1,0:T(8,128)} %weight_ref.1) | copy-start | bytes 786436
  6.1 0.7 copy-start.4
  6.7 0.7 copy-start.5

commit v2 on v1

v2 whole, which is shorter than its diff:
```python
import functools
import math

import jax
import jax.numpy as jnp
from jax import lax
from jax.experimental import pallas as pl
from jax.experimental.pallas import tpu as pltpu
from jax.sharding import PartitionSpec as P

MESH = pl.DeviceIdType.MESH
F32, BF16, I32 = jnp.float32, jnp.bfloat16, jnp.int32
PARTS = 2
SUBS = 2


def split(value):
    high = value.astype(BF16)
    return high, (value - high.astype(F32)).astype(BF16)


def wide(value):
    return jnp.concatenate(split(value), axis=1)


def mm(a, b, dims=((1,), (0,))):
    return lax.dot_general(a, b, (dims, ((), ())), preferred_element_type=F32)


def mm3(a, b, dims=((1,), (0,))):
    return mm(a[0], b[0], dims) + mm(a[1], b[0], dims) + mm(a[0], b[1], dims)


def each(start, stop, body):
    if stop - start <= 8:
        for i in range(start, stop):
            body(i)
    else:

        def step(i, carry):
            body(i)
            return carry

        lax.fori_loop(start, stop, step, 0)


def partners(n, body):
    if n <= 8:
        for k in sorted(range(1, n), key=lambda k: abs(2 * k - n)):
            body(k)
    else:
        each(1, n, body)


def order_of(own, other, meta, base):
    count = own.shape[1]
    row_at = lax.broadcasted_iota(I32, (count, count), 0)
    lane_at = lax.broadcasted_iota(I32, (count, count), 1)

    def upright(v):
        return jnp.sum(jnp.where(row_at == lane_at, jnp.broadcast_to(v, row_at.shape), 0), axis=1, keepdims=True)

    own_up, other_up = upright(own), upright(other)
    before = (own < own_up) | ((own == own_up) & (lane_at < row_at))
    rank = jnp.sum(before.astype(I32), axis=1, keepdims=True)
    placed = rank == lane_at

    def lay(v):
        return jnp.sum(jnp.where(placed, v, 0), axis=0, keepdims=True)

    meta[base : base + 1, :count] = lay(row_at)
    meta[base + 1 : base + 2, :count] = lay(jnp.broadcast_to(own_up, row_at.shape))
    meta[base + 2 : base + 3, :count] = lay(jnp.broadcast_to(other_up, row_at.shape))
    meta[base + 3 : base + 4, :count] = jnp.maximum(
        jnp.sum((own_up <= lane_at).astype(I32), axis=0, keepdims=True) - 1, 0
    )
    meta[base + 4 : base + 5, :count] = jnp.sum((own_up == lane_at).astype(I32), axis=0, keepdims=True)


def kernel(
    sizes,
    features_hbm, weight_hbm, cotangent_hbm, column_hbm, rows_hbm, cols_hbm, edges_hbm,
    activated_ref, input_ref, wgrad_ref,
    feat, cot, weight_ref, column_ref, rows_ref, cols_ref, edges, edge_f, edge_b, meta, plan, onehot, onehot_t,
    send, recv, table, run, dest, near, mid, far, agg, pre, every, back, back_in,
    wpart, wrow, wsum, wcol, wown, wall,
    load_sem, a_send, a_recv, n_send, n_recv, g_send, g_recv, b_send, b_recv,
    wr_send, wr_recv, wz_send, wz_recv, wy_send, wy_recv, wx_send, wx_recv,
):
    n_row, n_col, cap, block, d_blocks, s_blocks, reducers = sizes
    count = edges.shape[0]
    rd, width = feat.shape
    half = width // PARTS
    row, col = lax.axis_index("row"), lax.axis_index("col")
    p1 = row + 1 - 2 * lax.rem(row, 2)
    p2 = lax.rem(row + 2, n_row)
    p3 = lax.rem(p1 + 2, n_row)

    def remote(src, dst, s_sem, r_sem, where):
        return pltpu.make_async_remote_copy(
            src_ref=src, dst_ref=dst, send_sem=s_sem, recv_sem=r_sem, device_id=where, device_id_type=MESH
        )

    barrier = pltpu.get_barrier_semaphore()
    each(1, n_row, lambda k: pl.semaphore_signal(
        barrier, inc=1, device_id={"row": lax.rem(row + k, n_row)}, device_id_type=MESH))
    each(1, n_col, lambda k: pl.semaphore_signal(
        barrier, inc=1, device_id={"col": lax.rem(col + k, n_col)}, device_id_type=MESH))

    load_f = pltpu.make_async_copy(features_hbm, feat, load_sem.at[0])
    load_e = pltpu.make_async_copy(edges_hbm, edges, load_sem.at[1])
    load_c = pltpu.make_async_copy(cotangent_hbm, cot, load_sem.at[2])
    load_t = pltpu.make_async_copy(column_hbm, column_ref, load_sem.at[4])
    load_r = pltpu.make_async_copy(rows_hbm, rows_ref, load_sem.at[5])
    load_l = pltpu.make_async_copy(cols_hbm, cols_ref, load_sem.at[6])
    load_w = pltpu.make_async_copy(weight_hbm, weight_ref, load_sem.at[7])
    load_t.start()
    load_f.start()
    load_r.start()
    load_l.start()
    load_w.start()
    load_e.start()
    load_c.start()

    same = lax.broadcasted_iota(I32, (rd, rd), 1) == lax.broadcasted_iota(I32, (rd, rd), 0)
    load_t.wait()
    target = jnp.sum(jnp.where(same, jnp.broadcast_to(column_ref[...], (rd, rd)), 0), axis=1, keepdims=True)
    named = lax.broadcasted_iota(I32, (rd, 128), 1) == target
    below = lax.broadcasted_iota(I32, (rd, rd), 1) < lax.broadcasted_iota(I32, (rd, rd), 0)
    earlier = mm(below.astype(F32).astype(BF16), named.astype(F32).astype(BF16))
    rank = jnp.sum(jnp.where(named, earlier, 0.0), axis=1, keepdims=True)
    slot = target * cap + rank.astype(I32)
    slot_row = jnp.sum(jnp.where(same, jnp.broadcast_to(slot, (rd, rd)), 0), axis=0, keepdims=True)
    slots = n_col * cap
    onehot[...] = (lax.broadcasted_iota(I32, (slots, rd), 0) == slot_row).astype(F32).astype(BF16)
    load_f.wait()

    def route_copy(part, k):
        to = lax.rem(col + k, n_col)
        return remote(
            send.at[part, pl.ds(pl.multiple_of(to * cap, cap), cap)],
            recv.at[part, pl.ds(pl.multiple_of(col * cap, cap), cap)],
            a_send.at[part, to], a_recv.at[part, col], {"col": to},
        )

    def route_arrival(part, k):
        of = lax.rem(col + k, n_col)
        return remote(
            send.at[part, pl.ds(pl.multiple_of(of * cap, cap), cap)],
            recv.at[part, pl.ds(pl.multiple_of(of * cap, cap), cap)],
            a_send.at[part, of], a_recv.at[part, of], {"col": of},
        )

    mine = pl.ds(pl.multiple_of(col * cap, cap), cap)
    for part in range(PARTS):
        both = mm(onehot[...], wide(feat[:, part * half : (part + 1) * half]))
        send[part] = both[:, :half] + both[:, half:]
        if part == 0:
            pl.semaphore_wait(barrier, n_row + n_col - 2)
        partners(n_col, lambda k: route_copy(part, k).start())
        recv[part, mine] = send[part, mine]

    load_r.wait()
    load_l.wait()
    order_of(rows_ref[...], cols_ref[...], meta, 0)
    order_of(cols_ref[...], rows_ref[...], meta, 8)
    load_m = pltpu.make_async_copy(meta, plan, load_sem.at[3])
    load_m.start()
    onehot_t[...] = (lax.broadcasted_iota(I32, (rd, slots), 1) == slot).astype(F32).astype(BF16)
    load_e.wait()

    def prepare(k, carry):
        value = edges[k]
        edge_f[k] = wide(value)
        edge_b[k] = wide(value.T)
        return carry

    lax.fori_loop(0, count, prepare, 0)
    load_m.wait()
    load_c.wait()
    load_w.wait()
    w_pair = split(weight_ref[...])

    def fill(at, value):
        pair = wide(value)
        table[at, :block] = pair
        table[at, block:] = pair

    def multiply(edge_ref, base):
        def step(p, total):
            product = mm(edge_ref[plan[base, p]], table[plan[base + 2, p]])
            kept = plan[base + 1, p] == plan[base + 1, jnp.maximum(p - 1, 0)]
            total = jnp.where(kept, total, 0.0) + product[:, :half] + product[:, half:]
            run[p] = total
            return total

        lax.fori_loop(0, count, step, jnp.zeros((block, half), F32), unroll=8)

    def taken(base, at):
        return jnp.where(plan[base + 4, at] > 0, run[plan[base + 3, at]], 0.0)

    per = rd // block

    sub = rd // SUBS
    per_sub = per // SUBS

    def near_copy(part, which, at):
        rows = slice(at * sub, (at + 1) * sub)
        return remote(
            dest.at[part, p3 if which == 0 else p1, rows], near.at[part, which, rows],
            n_send.at[part, which, at], n_recv.at[part, which, at], {"row": p1},
        )

    def far_copy(part, at):
        rows = slice(at * sub, (at + 1) * sub)
        return remote(
            mid.at[part, rows], far.at[part, rows], n_send.at[part, 2, at], n_recv.at[part, 2, at], {"row": p2}
        )

    for part in range(PARTS):
        partners(n_col, lambda k: route_arrival(part, k).wait_recv())
        for s in range(s_blocks):
            fill(s, recv[part, s * block : (s + 1) * block])
        multiply(edge_f, 0)
        for which, owner in enumerate((p3, p2, p1, row)):
            for at in range(SUBS):
                for i in range(at * per_sub, (at + 1) * per_sub):
                    dest[part, owner, i * block : (i + 1) * block] = taken(0, owner * per + i)
                if which == 0:
                    near_copy(part, 0, at).start()
                if which == 2:
                    near_copy(part, 1, at).start()
            if which == 1:
                for at in range(SUBS):
                    rows = slice(at * sub, (at + 1) * sub)
                    near_copy(part, 0, at).wait_recv()
                    mid[part, rows] = dest[part, p2, rows] + near[part, 0, rows]
                    far_copy(part, at).start()

    def give(part, which, at):
        owner, rows = row if which < 2 else p2, slice(at * sub, (at + 1) * sub)
        return remote(
            every.at[part, owner, rows], every.at[part, owner, rows],
            g_send.at[part, which, at], g_recv.at[part, which, at], {"row": p2 if which == 0 else p1},
        )

    def take(part, which, at):
        owner, rows = (p2, p1, p3)[which], slice(at * sub, (at + 1) * sub)
        return remote(
            every.at[part, owner, rows], every.at[part, owner, rows],
            g_send.at[part, which, at], g_recv.at[part, which, at], {"row": p2 if which == 0 else p1},
        )

    scale = math.sqrt(2.0 / math.pi)
    for at in range(SUBS):
        rows = slice(at * sub, (at + 1) * sub)
        for part in range(PARTS):
            near_copy(part, 1, at).wait_recv()
            far_copy(part, at).wait_recv()
            agg[rows, part * half : (part + 1) * half] = (
                dest[part, row, rows] + near[part, 1, rows] + far[part, rows]
            )
        x = mm3(split(agg[rows]), w_pair)
        square = x * x
        t = jnp.tanh(scale * (x + 0.044715 * (square * x)))
        activated_ref[rows] = 0.5 * x * (1.0 + t)
        slope = 0.5 * (1.0 + t) + 0.5 * x * (1.0 - t * t) * (scale * (1.0 + 3.0 * 0.044715 * square))
        pre[rows] = cot[rows] * slope
        grad = mm3(split(pre[rows]), w_pair, ((1,), (1,)))
        for part in range(PARTS):
            every[part, row, rows] = grad[:, part * half : (part + 1) * half]
        give(0, 0, at).start()
        give(0, 1, at).start()
    for part in range(1, PARTS):
        for at in range(SUBS):
            give(part, 0, at).start()
            give(part, 1, at).start()

    def back_copy(part, k):
        to = lax.rem(col + k, n_col)
        return remote(
            back.at[part, pl.ds(pl.multiple_of(to * cap, cap), cap)],
            back_in.at[part, pl.ds(pl.multiple_of(col * cap, cap), cap)],
            b_send.at[part, to], b_recv.at[part, col], {"col": to},
        )

    def back_arrival(part, k):
        of = lax.rem(col + k, n_col)
        return remote(
            back.at[part, pl.ds(pl.multiple_of(of * cap, cap), cap)],
            back_in.at[part, pl.ds(pl.multiple_of(of * cap, cap), cap)],
            b_send.at[part, of], b_recv.at[part, of], {"col": of},
        )

    piece = width // reducers
    share = piece // n_row

    def w_col_copy(to):
        return remote(wpart.at[to], wcol.at[col], wz_send.at[to], wz_recv.at[col], {"col": to})

    def w_col_arrival(of):
        return remote(wpart.at[0], wcol.at[of], wz_send.at[0], wz_recv.at[of], {"col": of})

    def w_row_copy(k):
        to = lax.rem(row + k, n_row)
        return remote(wsum.at[to], wrow.at[row], wr_send.at[to], wr_recv.at[row], {"row": to})

    def w_row_arrival(k):
        of = lax.rem(row + k, n_row)
        return remote(wsum.at[of], wrow.at[of], wr_send.at[of], wr_recv.at[of], {"row": of})

    def w_col_give(k):
        to = lax.rem(col + k, n_col)
        return remote(wown, wall.at[row, col], wy_send.at[to], wy_recv.at[col], {"col": to})

    def w_col_take(of):
        return remote(wown, wall.at[row, of], wy_send.at[of], wy_recv.at[of], {"col": of})

    def w_row_give(k):
        to = lax.rem(row + k, n_row)
        return remote(wall.at[row], wall.at[row], wx_send.at[to], wx_recv.at[row], {"row": to})

    def w_row_take(k):
        of = lax.rem(row + k, n_row)
        return remote(wall.at[of], wall.at[of], wx_send.at[of], wx_recv.at[of], {"row": of})

    def reducer(body):
        if reducers == n_col:
            body()
        else:
            pl.when(col < reducers)(body)

    def others(body):
        if reducers == n_col:
            partners(n_col, lambda k: body(lax.rem(col + k, n_col)))
        else:
            each(0, reducers, lambda j: pl.when(col != j)(lambda: body(j)))

    def w_first():
        wlocal = mm3(split(agg[...]), split(pre[...]), ((0,), (0,)))
        for j in range(reducers):
            wpart[j] = wlocal[j * piece : (j + 1) * piece]
        others(lambda j: w_col_copy(j).start())

    def w_second():
        partners(n_col, lambda k: w_col_arrival(lax.rem(col + k, n_col)).wait_recv())
        wcol[col] = wpart[col]
        total = wcol[0]
        for j in range(1, n_col):
            total = total + wcol[j]
        for r in range(n_row):
            wsum[r] = total[r * share : (r + 1) * share]
        each(1, n_row, lambda k: w_row_copy(k).start())

    def w_third():
        each(1, n_row, lambda k: w_row_arrival(k).wait_recv())
        wrow[row] = wsum[row]
        total = wrow[0]
        for r in range(1, n_row):
            total = total + wrow[r]
        wown[...] = total * (float(rd * n_row * n_col) ** -0.5)
        each(1, n_col, lambda k: w_col_give(k).start())
        wall[row, col] = wown[...]

    def w_fourth():
        others(lambda j: w_col_take(j).wait_recv())
        each(1, n_row, lambda k: w_row_give(k).start())

    w_first()
    for part in range(PARTS):
        for at in range(SUBS):
            take(part, 0, at).wait_recv()
            give(part, 2, at).start()
        if part == 1:
            reducer(w_third)
        for which, owner in ((3, row), (1, p1), (0, p2), (2, p3)):
            for at in range(SUBS):
                if which in (1, 2):
                    take(part, which, at).wait_recv()
                for i in range(at * per_sub, (at + 1) * per_sub):
                    fill(owner * per + i, every[part, owner, i * block : (i + 1) * block])
        multiply(edge_b, 8)
        for s in range(s_blocks):
            back[part, s * block : (s + 1) * block] = taken(8, s)
        partners(n_col, lambda k: back_copy(part, k).start())
        back_in[part, mine] = back[part, mine]
        if part == 0:
            reducer(w_second)

    for part in range(PARTS):
        partners(n_col, lambda k: back_arrival(part, k).wait_recv())
        both = mm(onehot_t[...], wide(back_in[part]))
        input_ref[:, part * half : (part + 1) * half] = both[:, :half] + both[:, half:]
        if part == 0:
            w_fourth()
    each(1, n_row, lambda k: w_row_take(k).wait_recv())
    for r in range(n_row):
        for j in range(reducers):
            wgrad_ref[j * piece + r * share : j * piece + (r + 1) * share] = wall[r, j]

    for part in range(PARTS):
        partners(n_col, lambda k: route_copy(part, k).wait_send())
        partners(n_col, lambda k: back_copy(part, k).wait_send())
        for at in range(SUBS):
            near_copy(part, 0, at).wait_send()
            near_copy(part, 1, at).wait_send()
            far_copy(part, at).wait_send()
            for which in range(3):
                give(part, which, at).wait_send()
    others(lambda j: w_col_copy(j).wait_send())

    def last():
        each(1, n_row, lambda k: w_row_copy(k).wait_send())
        each(1, n_col, lambda k: w_col_give(k).wait_send())

    reducer(last)
    each(1, n_row, lambda k: w_row_give(k).wait_send())


def local(n_row, n_col, features, weight, cotangent, column_of, block_rows, block_cols, edge_blocks):
    rd, width = features.shape
    count, block = edge_blocks.shape[1:3]
    cap = max(2, 2 * rd // n_col)
    slots = n_col * cap
    d_blocks, s_blocks = n_row * rd // block, slots // block
    half = width // PARTS
    reducers = min(n_col, width // (8 * n_row))
    piece = width // reducers
    share = piece // n_row
    sizes = (n_row, n_col, cap, block, d_blocks, s_blocks, reducers)
    vmem = pl.BlockSpec(memory_space=pltpu.VMEM)
    hbm = pl.BlockSpec(memory_space=pltpu.HBM)
    V, D = pltpu.VMEM, pltpu.SemaphoreType.DMA
    return pl.pallas_call(
        functools.partial(kernel, sizes),
        out_shape=(
            jax.ShapeDtypeStruct((rd, width), F32),
            jax.ShapeDtypeStruct((rd, width), F32),
            jax.ShapeDtypeStruct((width, width), F32),
        ),
        in_specs=[hbm] * 7,
        out_specs=(vmem, vmem, vmem),
        scratch_shapes=[
            V((rd, width), F32),
            V((rd, width), F32),
            V((width, width), F32),
            V((1, rd), I32),
            V((1, count), I32),
            V((1, count), I32),
            V((count, block, block), F32),
            V((count, block, 2 * block), BF16),
            V((count, block, 2 * block), BF16),
            V((16, 128), I32),
            pltpu.SMEM((16, 128), I32),
            V((slots, rd), BF16),
            V((rd, slots), BF16),
            V((PARTS, slots, half), F32),
            V((PARTS, slots, half), F32),
            V((max(d_blocks, s_blocks), 2 * block, 2 * half), BF16),
            V((count, block, half), F32),
            V((PARTS, n_row, rd, half), F32),
            V((PARTS, 2, rd, half), F32),
            V((PARTS, rd, half), F32),
            V((PARTS, rd, half), F32),
            V((rd, width), F32),
            V((rd, width), F32),
            V((PARTS, n_row, rd, half), F32),
            V((PARTS, slots, half), F32),
            V((PARTS, slots, half), F32),
            V((reducers, piece, width), F32),
            V((n_row, share, width), F32),
            V((n_row, share, width), F32),
            V((n_col, piece, width), F32),
            V((share, width), F32),
            V((n_row, reducers, share, width), F32),
            D((8,)),
            D((PARTS, n_col)), D((PARTS, n_col)),
            D((PARTS, 3, SUBS)), D((PARTS, 3, SUBS)),
            D((PARTS, 3, SUBS)), D((PARTS, 3, SUBS)),
            D((PARTS, n_col)), D((PARTS, n_col)),
            D((n_row,)), D((n_row,)),
            D((n_col,)), D((n_col,)),
            D((n_col,)), D((n_col,)),
            D((n_row,)), D((n_row,)),
        ],
        compiler_params=pltpu.CompilerParams(
            collective_id=0, has_side_effects=True, vmem_limit_bytes=60 * 2**20
        ),
    )(features, weight, cotangent, column_of.reshape(1, rd), block_rows, block_cols, edge_blocks[0])


def solution(mesh):
    spread = P(("groups", "row", "col"), None)
    placed = (spread, P(), spread, spread, spread, spread, P(("groups", "row", "col"), None, None, None))
    return jax.shard_map(
        functools.partial(local, mesh.shape["row"], mesh.shape["col"]),
        mesh=mesh,
        in_specs=placed,
        out_specs=(spread, spread, P("groups", None)),
        check_vma=False,
    )
```

time: 91.1 us -> 77.7 us (0.85)
  Pallas kernels: 80.3 us -> 72.2 us
  local copies, waits for them, and re-layouts: 9.04 us -> 4.48 us
    pallas_call x1, Pallas kernels: 80.3 us -> 72.2 us  [local(): pl.pallas_call(functools.partial(kernel, sizes), out_shape=(jax.ShapeDtyp...]
    unnamed x16 -> x5, local copies, waits for them, and re-layouts: 9.04 us -> 4.48 us
where the time goes in v2:
time: 77.7 us; the launch traced here: 77.4 us
  Pallas kernels  72.2 us (93%)
  local copies, waits for them, and re-layouts  4.48 us (6%)
    pallas_call x1, Pallas kernels, local(): pl.pallas_call(functools.partial(kernel, sizes), out_shape=(jax.ShapeDtyp...  72.2 us
    unnamed x5, local copies, waits for them, and re-layouts  4.48 us

profile of v2, /device:TPU:1, one launch (start us, length us, event | category | flops | bytes accessed | tf_op | source)
XLA Modules:
  0.0 77.4 jit_solution(13131025451993745310)
XLA Ops:
  0.6 72.2 %shard_map.94 = (f32[512,256]{1,0:T(8,128)}, f32[512,256]{1,0:T(8,128)}, f32[256,256]{1,0:T(8,128)}) custom-call(f32[512,256]{1,0:T(8,128)} %features_hbm.1, f32[256,256]{1,0:T(8,128)} %weight_hbm.1, f32[512,256]{1,0:T(8,128)} %cotangent_hbm.1, s32[1,512]{1,0:T(1,128)} %bitcast.3, s32[1,32]{1,0:T(1,128)} %rows_hbm.1, s32[1,32]{1,0:T(1,128)} %cols_hbm.1, ...), custom_call_target="tpu_custom_call" | custom-call | tf_op jit(solution)/shard_map/pallas_call | solution.py:434
  72.9 0.0 copy-start
  72.9 1.9 %copy.13 = f32[512,256]{1,0:T(8,128)} copy(f32[512,256]{1,0:T(8,128)} %get-tuple-element.6) | data formatting | bytes 1048576
  74.8 1.9 %copy.14 = f32[512,256]{1,0:T(8,128)} copy(f32[512,256]{1,0:T(8,128)} %get-tuple-element.7) | data formatting | bytes 1048576
  76.7 0.0 copy-done
  76.7 0.7 copy.15
Async XLA Ops:
  72.9 3.8 %copy-start = (f32[256,256]{1,0:T(8,128)S(1)}, f32[256,256]{1,0:T(8,128)}, u32[]{:S(2)}) copy-start(f32[256,256]{1,0:T(8,128)} %get-tuple-element.8) | copy-start | bytes 786436
